TPU v7x, 32 devices: a whole 2x2x4 slice. The times are simulated.
32 devices in a mesh: mp: 2 (over x), lat: 8 (over z, y), lon: 2 (over core).
Axes of the slice: x: 2, y: 2, z: 4, core: 2. Of those that a mesh axis runs over, the one named last changes fastest.
Arguments:
- state: bfloat16 [2, 160, 128, 1536], P('mp', None, 'lat', 'lon'), may hold values from -6 to 6
- conv_first: bfloat16 [2, 3, 3, 160, 160], P('mp'), may hold values from -0.15625 to 0.15625
- bias_first: float32 [2, 160], P('mp'), may hold values from -3 to 3
- conv_second: bfloat16 [2, 3, 3, 160, 160], P('mp'), may hold values from -0.15625 to 0.15625
- bias_second: float32 [2, 160], P('mp'), may hold values from -3 to 3
- norm_gain: float32 [2, 160], P('mp'), may hold values from 0.1 to 1.9
- export_weight: bfloat16 [2, 160, 8], P('mp'), may hold values from -0.5 to 0.5
- import_weight: bfloat16 [2, 8, 160], P('mp'), may hold values from -2 to 2
- regrid_rows: int32 [2, 128, 4], P('mp', 'lat'), may hold values from 0 to 127, as said below
- regrid_weights: float32 [2, 128, 4], P('mp', 'lat'), may hold values from 0.2 to 1
- sea_mask: int32 [2, 128, 1536], P('mp', 'lat', 'lon'), may hold values 0 or 1
Outputs:
- coupled: bfloat16 [2, 160, 128, 1536], P('mp', None, 'lat', 'lon')
Inputs may be any that keep to these rules, and one draw needn't show every extreme that they name: `regrid_rows`: the source rows of destination row d lie within 16 rows of d, and the first of them is row d itself.
All inputs are finite; a program needn't handle non-finite values. No bound on the sum of `sea_mask` on one device may be relied on, other than what follows from the above.
Results may differ from a plain program's by a relative error of at most 0.0065.
Values may be sent and summed in bfloat16 or wider, within the bound.
A program may use at most 192 MiB of HBM per device.

v0:
```python
import functools

import jax
import jax.numpy as jnp
from jax import lax
from jax.experimental import pallas as pl
from jax.experimental.pallas import tpu as pltpu
from jax.sharding import PartitionSpec as P

F32 = jnp.float32
BF16 = jnp.bfloat16
LANES = 128
SIDE = 64
VMEM_LIMIT = 58 * 1024 * 1024


def lane_of(shape):
    return lax.broadcasted_iota(jnp.int32, shape, 1)


def stacked_rows(edge):
    return jnp.concatenate(
        [pltpu.roll(edge, 1, 1), edge, pltpu.roll(edge, LANES - 1, 1)], axis=0
    ).astype(BF16)


def edge_terms(weights, edge):
    ch = edge.shape[0]
    taps = jnp.dot(weights, stacked_rows(edge), preferred_element_type=F32)
    return jnp.where(lane_of((ch, LANES)) < SIDE, taps[:ch], taps[2 * ch :])


def conv_row(weights, rows3, edges, row, offset):
    ch, width = edges.shape[0], rows3.shape[1]
    taps = jnp.dot(weights, rows3, preferred_element_type=F32)
    at = lane_of((ch, LANES))
    left = jnp.sum(jnp.where(at == row + 2, edges, 0.0), axis=1, keepdims=True)
    right = jnp.sum(jnp.where(at == row + 2 + SIDE, edges, 0.0), axis=1, keepdims=True)
    lane = lane_of((ch, width))
    west = jnp.where(lane == 0, left, pltpu.roll(taps[:ch], 1, 1))
    east = jnp.where(lane == width - 1, right, pltpu.roll(taps[2 * ch :], width - 1, 1))
    return taps[ch : 2 * ch] + west + east + offset


def silu(u):
    return u / (1.0 + jnp.exp(-u))


def first_kernel(x_ref, w_ref, b_ref, e_ref, xr_ref, hf_ref, flat, edges):
    ch, rows, width = x_ref.shape
    for j in range(width // LANES):
        flat[j] = x_ref[:, :, j * LANES : (j + 1) * LANES].astype(F32).reshape(ch * rows, LANES)
    for r in range(rows):
        for j in range(width // LANES):
            xr_ref[r * ch : (r + 1) * ch, j * LANES : (j + 1) * LANES] = flat.at[j][
                pl.ds(r, ch, stride=rows), :
            ].astype(BF16)
    edges[...] = edge_terms(w_ref[...], e_ref[...])

    @pl.loop(1, rows - 1)
    def _(r):
        rows3 = xr_ref[pl.ds(pl.multiple_of((r - 1) * ch, 16), 3 * ch), :]
        u = conv_row(w_ref[...], rows3, edges[...], r, b_ref[...])
        hf_ref[pl.ds(pl.multiple_of((r - 1) * ch, 16), ch), :] = silu(u).astype(BF16)


def second_kernel(
    ok_ref, xr_ref, top_ref, bot_ref, hf_ref, w1_ref, b1_ref, e_ref, w2_ref, b2_ref, g_ref,
    ex_ref, hid_ref, face_ref, xe, hfe, edges1, edges2,
):
    ch = g_ref.shape[0]
    width = xr_ref.shape[1]
    rows = xr_ref.shape[0] // ch
    xe[0, : 2 * ch] = top_ref[...]
    xe[0, 2 * ch :] = xr_ref[: 2 * ch]
    xe[1, : 2 * ch] = xr_ref[(rows - 2) * ch :]
    xe[1, 2 * ch :] = bot_ref[...]
    hfe[0, 2 * ch :] = hf_ref[: 2 * ch]
    hfe[1, : 2 * ch] = hf_ref[(rows - 4) * ch :]

    edges1[...] = edge_terms(w1_ref[...], e_ref[ch : 2 * ch])
    column = None
    for k in range(3):
        term = jnp.dot(
            w1_ref[k * ch : (k + 1) * ch],
            stacked_rows(e_ref[k * ch : (k + 1) * ch]),
            preferred_element_type=F32,
        )
        column = term if column is None else column + term
    column = silu(column + b1_ref[...])
    lane = lane_of((ch, LANES))
    lane = jnp.where(lane >= SIDE, lane - SIDE, lane)
    column = jnp.where((lane == 1) & (ok_ref[0] == 0), 0.0, column)
    column = jnp.where((lane == rows + 2) & (ok_ref[1] == 0), 0.0, column)
    column = jnp.where((lane < 1) | (lane > rows + 2), 0.0, column)
    edges2[...] = edge_terms(w2_ref[...], column.astype(BF16).astype(F32))

    @pl.loop(0, 4)
    def _(q):
        side, k = q // 2, q % 2
        rows3 = xe[side, pl.ds(pl.multiple_of(k * ch, 16), 3 * ch), :]
        r = jnp.where(side == 0, k - 1, rows - 1 + k)
        u = silu(conv_row(w1_ref[...], rows3, edges1[...], r, b1_ref[...]))
        gone = ((r < 0) & (ok_ref[0] == 0)) | ((r >= rows) & (ok_ref[1] == 0))
        u = jnp.where(gone, 0.0, u)
        hfe[side, pl.ds(pl.multiple_of((k + 2 * side) * ch, 16), ch), :] = u.astype(BF16)

    def finish(rows3, r):
        here = pl.ds(pl.multiple_of(r * ch, 16), ch)
        u = conv_row(w2_ref[...], rows3, edges2[...], r, b2_ref[...])
        u = u + xr_ref[here, :].astype(F32)
        mean = jnp.sum(u * u, axis=0, keepdims=True) * (1.0 / ch)
        h = (u * lax.rsqrt(mean + 1e-06) * g_ref[...]).astype(BF16)
        hid_ref[here, :] = h
        face_ref[r] = jnp.dot(ex_ref[...], h, preferred_element_type=F32).astype(BF16)

    @pl.loop(0, 4)
    def _(q):
        side, k = q // 2, q % 2
        rows3 = hfe[side, pl.ds(pl.multiple_of(k * ch, 16), 3 * ch), :]
        finish(rows3, jnp.where(side == 0, k, rows - 2 + k))

    @pl.loop(2, rows - 2)
    def _(r):
        finish(hf_ref[pl.ds(pl.multiple_of((r - 2) * ch, 16), 3 * ch), :], r)


def third_kernel(
    rows_ref, weights_ref, hid_ref, up_ref, mid_ref, down_ref, im_ref, mask_ref, out_ref, band, flat
):
    ch, step, width = out_ref.shape
    rows = up_ref.shape[0]
    base = pl.program_id(0) * step
    band[:rows] = up_ref[...].astype(F32)
    band[rows : 2 * rows] = mid_ref[...].astype(F32)
    band[2 * rows :] = down_ref[...].astype(F32)
    for d in range(step):
        total = None
        for k in range(rows_ref.shape[1]):
            term = weights_ref[base + d, k] * band[rows_ref[base + d, k]]
            total = term if total is None else total + term
        mixed = jnp.dot(im_ref[...], total.astype(BF16), preferred_element_type=F32)
        h = hid_ref[d * ch : (d + 1) * ch, :].astype(F32)
        value = h + mask_ref[d : d + 1, :].astype(F32) * mixed
        for j in range(width // LANES):
            flat.at[j][pl.ds(d, ch, stride=step), :] = value[:, j * LANES : (j + 1) * LANES]
    for j in range(width // LANES):
        out_ref[:, :, j * LANES : (j + 1) * LANES] = (
            flat[j].reshape(ch, step, LANES).astype(BF16)
        )


def vmem():
    return pl.BlockSpec(memory_space=pltpu.VMEM)


def smem():
    return pl.BlockSpec(memory_space=pltpu.SMEM)


def params():
    return pltpu.CompilerParams(vmem_limit_bytes=VMEM_LIMIT)


def both_ways(tail, head, axis):
    n = lax.axis_size(axis)
    return (
        lax.ppermute(tail, axis, [(i, i + 1) for i in range(n - 1)]),
        lax.ppermute(head, axis, [(i + 1, i) for i in range(n - 1)]),
    )


def on_device(
    state, conv_first, bias_first, conv_second, bias_second, norm_gain, export_weight,
    import_weight, regrid_rows, regrid_weights, sea_mask,
):
    source = state[0]
    ch, rows, width = source.shape
    lat = lax.axis_index("lat")
    n_lat = lax.axis_size("lat")

    def row_block(part):
        return part.transpose(1, 0, 2).reshape(-1, width)

    top, bot = both_ways(
        row_block(source[:, rows - 2 :]), row_block(source[:, :2]), "lat"
    )
    own = jnp.stack([source[:, :, i] for i in (0, 1, width - 2, width - 1)])
    far = lax.ppermute(own, "lon", [(0, 1), (1, 0)])
    cols = jnp.concatenate([far[2:4], own[0:1], own[3:4], far[0:2]])
    above, below = both_ways(cols[:, :, rows - 2 :], cols[:, :, :2], "lat")

    def in_lanes(cols, first_row):
        before = first_row + 2
        cols = jnp.pad(cols, ((0, 0), (0, 0), (before, SIDE - before - cols.shape[2])))
        return jnp.concatenate([cols[:3], cols[3:]], axis=2).reshape(3 * ch, LANES).astype(F32)

    edge_own = in_lanes(cols, 0)[ch : 2 * ch]
    edge_all = in_lanes(jnp.concatenate([above, cols, below], axis=2), -2)

    def taps(kernel):
        return kernel.transpose(1, 3, 0, 2).reshape(3 * ch, 3 * ch)

    w1, w2 = taps(conv_first[0]), taps(conv_second[0])
    b1, b2, gain = bias_first[0][:, None], bias_second[0][:, None], norm_gain[0][:, None]

    per_row = 2 * 9 * ch * ch * width
    xr, hf = pl.pallas_call(
        first_kernel,
        name="conv_first_inner",
        out_shape=(
            jax.ShapeDtypeStruct((rows * ch, width), BF16),
            jax.ShapeDtypeStruct(((rows - 2) * ch, width), BF16),
        ),
        in_specs=[vmem()] * 4,
        out_specs=(vmem(), vmem()),
        scratch_shapes=[
            pltpu.VMEM((width // LANES, rows * ch, LANES), F32),
            pltpu.VMEM((ch, LANES), F32),
        ],
        compiler_params=params(),
        cost_estimate=pl.CostEstimate(
            flops=per_row * (rows - 2), bytes_accessed=6 * rows * ch * width, transcendentals=0
        ),
    )(source, w1, b1, edge_own)

    ok = jnp.stack([lat > 0, lat < n_lat - 1]).astype(jnp.int32)
    n_face = export_weight.shape[2]
    hidden, face = pl.pallas_call(
        second_kernel,
        name="conv_second",
        out_shape=(
            jax.ShapeDtypeStruct((rows * ch, width), BF16),
            jax.ShapeDtypeStruct((rows, n_face, width), BF16),
        ),
        in_specs=[smem()] + [vmem()] * 11,
        out_specs=(vmem(), vmem()),
        scratch_shapes=[
            pltpu.VMEM((2, 4 * ch, width), BF16),
            pltpu.VMEM((2, 4 * ch, width), BF16),
            pltpu.VMEM((ch, LANES), F32),
            pltpu.VMEM((ch, LANES), F32),
        ],
        compiler_params=params(),
        cost_estimate=pl.CostEstimate(
            flops=per_row * (rows + 4), bytes_accessed=6 * rows * ch * width, transcendentals=0
        ),
    )(ok, xr, top, bot, hf, w1, b1, edge_all, w2, b2, gain, export_weight[0].T)

    mid = lax.ppermute(face, "mp", [(0, 1), (1, 0)])
    up, down = both_ways(mid, mid, "lat")
    weights = regrid_weights[0]
    normed = weights / jnp.sum(weights, axis=1, keepdims=True)
    local_rows = regrid_rows[0] - (lat - 1) * rows

    step = 8
    whole = lambda shape: pl.BlockSpec(shape, lambda i: (0,) * len(shape))
    out = pl.pallas_call(
        third_kernel,
        name="exchange",
        grid=(rows // step,),
        out_shape=jax.ShapeDtypeStruct((ch, rows, width), BF16),
        in_specs=[
            smem(),
            smem(),
            pl.BlockSpec((step * ch, width), lambda i: (i, 0)),
            whole(mid.shape),
            whole(mid.shape),
            whole(mid.shape),
            whole((ch, n_face)),
            pl.BlockSpec((step, width), lambda i: (i, 0)),
        ],
        out_specs=pl.BlockSpec((ch, step, width), lambda i: (0, i, 0)),
        scratch_shapes=[
            pltpu.VMEM((3 * rows, n_face, width), F32),
            pltpu.VMEM((width // LANES, step * ch, LANES), F32),
        ],
        compiler_params=params(),
    )(local_rows, normed, hidden, up, mid, down, import_weight[0].T, sea_mask[0])
    return out[None]


def solution(mesh):
    return jax.shard_map(
        on_device,
        mesh=mesh,
        in_specs=(
            P("mp", None, "lat", "lon"),
            P("mp", None, None, None, None),
            P("mp", None),
            P("mp", None, None, None, None),
            P("mp", None),
            P("mp", None),
            P("mp", None, None),
            P("mp", None, None),
            P("mp", "lat", None),
            P("mp", "lat", None),
            P("mp", "lat", "lon"),
        ),
        out_specs=P("mp", None, "lat", "lon"),
        check_vma=False,
    )
```

profile of v0, /device:TPU:0, one launch (start us, length us, event | category | flops | bytes accessed | tf_op | source)
XLA Modules:
  0.0 101.7 jit_solution(9941212973814668475)
XLA Ops:
  0.0 2.5 %fusion.2 = (bf16[160,16,1]{2,1,0:T(8,128)(2,1)S(1)}, bf16[160,16,1]{2,1,0:T(8,128)(2,1)S(1)}, bf16[160,16,1]{2,1,0:T(8,128)(2,1)S(1)}, bf16[160,16,1]{2,1,0:T(8,128)(2,1)S(1)}) fusion(bf16[160,16,768]{2,1,0:T(8,128)(2,1)} %bitcast.41), kind=kLoop, calls=%fused_computation.17 | loop fusion | bytes 40960 | tf_op jit(solution)/shard_map/slice | solution.py:188
  2.5 0.0 copy-start
  2.6 0.6 copy.76
  3.2 0.6 copy.73
  3.8 0.6 copy.75
  4.4 0.0 copy-start.8
  4.4 0.0 copy-start.1
  4.4 0.6 copy.74
  5.0 0.5 collective-permute-start
  5.5 2.9 %slice_bitcast_fusion = (bf16[2,160,768]{2,0,1:T(2,128)(2,1)S(1)}, bf16[2,160,768]{2,0,1:T(2,128)(2,1)S(1)}) fusion(bf16[160,16,768]{2,1,0:T(8,128)(2,1)} %bitcast.42), kind=kLoop, calls=%fused_computation | loop fusion | bytes 1966080 | tf_op jit(solution)/shard_map/transpose | solution.py:183
  8.4 0.1 copy.79
  8.5 0.0 copy-start.9
  8.5 0.0 copy-start.10
  8.5 5.2 %collective-permute-start.1 = (bf16[320,768]{1,0:T(8,128)(2,1)S(1)}, bf16[320,768]{1,0:T(8,128)(2,1)}, u32[]{:S(2)}, u32[]{:S(2)}) collective-permute-start(bf16[320,768]{1,0:T(8,128)(2,1)S(1)} %bitcast.46), channel_id=1, source_target_pairs={{0,2},{2,4},{4,6},{6,8},{8,10},{10,12},{12,14},{1,3},{3,5},{5,7},{... | collective-permute-start | bytes 1474568 | tf_op jit(solution)/shard_map/ppermute | solution.py:168
  13.7 0.8 copy.80
  14.6 1.3 %collective-permute-start.2 = (bf16[320,768]{1,0:T(8,128)(2,1)}, bf16[320,768]{1,0:T(8,128)(2,1)}, u32[]{:S(2)}, u32[]{:S(2)}) collective-permute-start(bf16[320,768]{1,0:T(8,128)(2,1)} %bitcast.16), channel_id=1, source_target_pairs={{2,0},{4,2},{6,4},{8,6},{10,8},{12,10},{14,12},{3,1},{5,3},{7,5},{... | collective-permute-start | bytes 1474568 | tf_op jit(solution)/shard_map/ppermute | solution.py:169
  15.9 0.6 add_convert_fusion.ok_ref
  16.5 0.0 copy-done
  16.5 0.9 copy.72
  17.4 1.3 %reshape.22.w_ref.w1_ref = bf16[480,480]{1,0:T(8,128)(2,1)} reshape(bf16[3,160,3,160]{3,2,1,0:T(4,128)(2,1)S(1)} %copy.72) | data formatting | bytes 921600 | tf_op jit(solution)/shard_map/reshape | solution.py:202
  18.7 0.0 copy-done.8
  18.7 0.8 copy.78.b_ref.b1_ref
  19.4 0.0 copy-done.1
  19.4 0.9 copy.82
  20.4 1.2 %reshape.25.w2_ref = bf16[480,480]{1,0:T(8,128)(2,1)} reshape(bf16[3,160,3,160]{3,2,1,0:T(4,128)(2,1)S(1)} %copy.82) | data formatting | bytes 921600 | tf_op jit(solution)/shard_map/reshape | solution.py:202
  21.6 0.0 copy-done.9
  21.6 0.7 copy.84.b2_ref
  22.3 0.0 copy-done.10
  22.3 0.7 copy.85.g_ref
  23.1 0.0 collective-permute-done
  23.1 0.2 copy.77
  23.3 4.5 %collective-permute-start.3 = (bf16[6,160,2]{1,2,0:T(2,128)(2,1)S(1)}, bf16[6,160,2]{1,2,0:T(2,128)(2,1)S(1)}, u32[]{:S(2)}, u32[]{:S(2)}) collective-permute-start(bf16[6,160,2]{1,2,0:T(2,128)(2,1)S(1)} %get-tuple-element.23), channel_id=1, source_target_pairs={{0,2},{2,4},{4,6},{6,8},{8,10},{10,12},{12,14},{1,3},{3,5},{5,7},{... | collective-permute-start | bytes 11528 | tf_op jit(solution)/shard_map/ppermute | solution.py:168
  27.9 1.5 %collective-permute-start.4 = (bf16[6,160,2]{1,2,0:T(2,128)(2,1)S(1)}, bf16[6,160,2]{1,2,0:T(2,128)(2,1)S(1)}, u32[]{:S(2)}, u32[]{:S(2)}) collective-permute-start(bf16[6,160,2]{1,2,0:T(2,128)(2,1)S(1)} %get-tuple-element.24), channel_id=1, source_target_pairs={{2,0},{4,2},{6,4},{8,6},{10,8},{12,10},{14,12},{3,1},{5,3},{7,5},{... | collective-permute-start | bytes 11528 | tf_op jit(solution)/shard_map/ppermute | solution.py:169
  29.3 0.1 pad_slice_fusion.3
  29.5 0.7 fusion.1.e_ref
  30.2 20.0 %conv_first_inner.1 = (bf16[2560,768]{1,0:T(8,128)(2,1)}, bf16[2240,768]{1,0:T(8,128)(2,1)}) custom-call(bf16[160,16,768]{2,1,0:T(8,128)(2,1)} %bitcast.43, bf16[480,480]{1,0:T(8,128)(2,1)} %reshape.22.w_ref.w1_ref, f32[160,1]{1,0:T(8,128)} %copy.78.b_ref.b1_ref, f32[160,128]{1,0:T(8,128)} %fusion.1.e_ref), custom_call_target="tpu_custom_call" | custom-call | flops 4954521600 | bytes 11796480 | tf_op jit(solution)/shard_map/conv_first_inner/pallas_call | solution.py:208
  50.2 0.0 collective-permute-done.3
  50.2 0.0 collective-permute-done.4
  50.2 0.2 copy.81
  50.4 0.1 pad_slice_fusion.1
  50.5 0.1 pad_maximum_fusion
  50.6 0.7 bitcast_convert_fusion.e_ref
  51.3 0.0 collective-permute-done.1.top_ref
  51.3 0.0 collective-permute-done.2.bot_ref
  51.3 0.0 copy-start.6
  51.3 0.0 copy-start.5
  51.4 24.7 %conv_second.1 = (bf16[2560,768]{1,0:T(8,128)(2,1)}, bf16[16,8,768]{2,1,0:T(8,128)(2,1)}) custom-call(s32[2]{0:T(128)} %add_convert_fusion.ok_ref, bf16[2560,768]{1,0:T(8,128)(2,1)} %get-tuple-element.9.xr_ref, bf16[320,768]{1,0:T(8,128)(2,1)} %collective-permute-done.1.top_ref, bf16[320,768]{1,0:T(8,128)(2,1)} %collective-permute-done.2.bot_ref, ...), custom_call_target="tpu_custom_call" | custom-call | flops 7077888000 | bytes 11796480 | tf_op jit(solution)/shard_map/conv_second/pallas_call | solution.py:229
  76.1 1.5 %collective-permute-start.5 = (bf16[16,8,768]{2,1,0:T(8,128)(2,1)}, bf16[16,8,768]{2,1,0:T(8,128)(2,1)S(1)}, u32[]{:S(2)}, u32[]{:S(2)}) collective-permute-start(bf16[16,8,768]{2,1,0:T(8,128)(2,1)} %get-tuple-element.12), channel_id=1, source_target_pairs={{0,16},{16,0},{1,17},{17,1},{2,18},{18,2},{3,19},{19,3},{4,20},{20... | collective-permute-start | bytes 589832 | tf_op jit(solution)/shard_map/ppermute | solution.py:250
  77.6 0.0 copy-done.7
  77.6 0.7 copy.87.rows_ref
  78.3 0.0 copy-done.6
  78.3 0.7 copy.86
  79.0 0.0 copy-done.5
  79.0 0.1 copy.70
  79.1 3.6 %collective-permute-done.5.mid_ref = bf16[16,8,768]{2,1,0:T(8,128)(2,1)S(1)} collective-permute-done((bf16[16,8,768]{2,1,0:T(8,128)(2,1)}, bf16[16,8,768]{2,1,0:T(8,128)(2,1)S(1)}, u32[]{:S(2)}, u32[]{:S(2)}) %collective-permute-start.5) | collective-permute-done | bytes 196640 | tf_op jit(solution)/shard_map/ppermute | solution.py:250
  82.7 4.3 %collective-permute-start.6 = (bf16[16,8,768]{2,1,0:T(8,128)(2,1)S(1)}, bf16[16,8,768]{2,1,0:T(8,128)(2,1)S(1)}, u32[]{:S(2)}, u32[]{:S(2)}) collective-permute-start(bf16[16,8,768]{2,1,0:T(8,128)(2,1)S(1)} %collective-permute-done.5.mid_ref), channel_id=1, source_target_pairs={{0,2},{2,4},{4,6},{6,8},{8,10},{10,12},{12,14},{1,3},{3,5},{5,7},{... | collective-permute-start | bytes 589832 | tf_op jit(solution)/shard_map/ppermute | solution.py:168
  87.0 1.3 %collective-permute-start.7 = (bf16[16,8,768]{2,1,0:T(8,128)(2,1)S(1)}, bf16[16,8,768]{2,1,0:T(8,128)(2,1)S(1)}, u32[]{:S(2)}, u32[]{:S(2)}) collective-permute-start(bf16[16,8,768]{2,1,0:T(8,128)(2,1)S(1)} %collective-permute-done.5.mid_ref), channel_id=1, source_target_pairs={{2,0},{4,2},{6,4},{8,6},{10,8},{12,10},{14,12},{3,1},{5,3},{7,5},{... | collective-permute-start | bytes 589832 | tf_op jit(solution)/shard_map/ppermute | solution.py:169
  88.3 0.7 broadcast_divide_fusion.weights_ref
  89.0 1.2 %collective-permute-done.6.up_ref = bf16[16,8,768]{2,1,0:T(8,128)(2,1)S(1)} collective-permute-done((bf16[16,8,768]{2,1,0:T(8,128)(2,1)S(1)}, bf16[16,8,768]{2,1,0:T(8,128)(2,1)S(1)}, u32[]{:S(2)}, u32[]{:S(2)}) %collective-permute-start.6) | collective-permute-done | bytes 196640 | tf_op jit(solution)/shard_map/ppermute | solution.py:168
  90.2 4.9 %collective-permute-done.7.down_ref = bf16[16,8,768]{2,1,0:T(8,128)(2,1)S(1)} collective-permute-done((bf16[16,8,768]{2,1,0:T(8,128)(2,1)S(1)}, bf16[16,8,768]{2,1,0:T(8,128)(2,1)S(1)}, u32[]{:S(2)}, u32[]{:S(2)}) %collective-permute-start.7) | collective-permute-done | bytes 196640 | tf_op jit(solution)/shard_map/ppermute | solution.py:169
  95.1 0.0 copy-done.2
  95.1 0.0 copy-done.3
  95.1 0.7 copy-done.4
  95.8 5.9 %exchange.1 = bf16[160,16,768]{2,1,0:T(8,128)(2,1)} custom-call(s32[16,4]{1,0:T(8,128)} %copy.87.rows_ref, f32[16,4]{1,0:T(8,128)} %broadcast_divide_fusion.weights_ref, bf16[2560,768]{1,0:T(8,128)(2,1)} %get-tuple-element.11.hid_ref, bf16[16,8,768]{2,1,0:T(8,128)(2,1)} %copy-done.3, bf16[16,8,768]{2,1,0:T(8,128)(2,1)} %copy-done.2, ...), custom_call_target="tpu_custom_call" | custom-call | tf_op jit(solution)/shard_map/exchange/pallas_call | solution.py:258
  (11 shorter events, 0.1 us)
Async XLA Ops:
  2.5 13.9 %copy-start = (bf16[1,3,3,160,160]{4,3,2,1,0:T(8,128)(2,1)S(1)}, bf16[1,3,3,160,160]{4,3,2,1,0:T(8,128)(2,1)}, u32[]{:S(2)}) copy-start(bf16[1,3,3,160,160]{4,3,2,1,0:T(8,128)(2,1)} %param.12) | copy-start | bytes 1382404
  4.4 14.3 %copy-start.8 = (f32[1,160]{1,0:T(1,128)S(1)}, f32[1,160]{1,0:T(1,128)}, u32[]{:S(2)}) copy-start(f32[1,160]{1,0:T(1,128)} %param.13) | copy-start | bytes 1924
  4.4 15.1 %copy-start.1 = (bf16[1,3,3,160,160]{4,3,2,1,0:T(8,128)(2,1)S(1)}, bf16[1,3,3,160,160]{4,3,2,1,0:T(8,128)(2,1)}, u32[]{:S(2)}) copy-start(bf16[1,3,3,160,160]{4,3,2,1,0:T(8,128)(2,1)} %param.14) | copy-start | bytes 1382404
  5.0 18.1 %collective-permute-start = (bf16[4,160,16]{1,2,0:T(8,128)(2,1)S(1)}, bf16[4,160,16]{1,2,0:T(8,128)(2,1)S(1)}, u32[]{:S(2)}, u32[]{:S(2)}) collective-permute-start(bf16[4,160,16]{1,2,0:T(8,128)(2,1)S(1)} %pad_maximum_fusion.4), channel_id=1, source_target_pairs={{0,1},{1,0},{2,3},{3,2},{4,5},{5,4},{6,7},{7,6},{8,9},{9,8},{10,11... | collective-permute-start | bytes 61448 | tf_op jit(solution)/shard_map/ppermute | solution.py:189
  8.5 13.1 %copy-start.9 = (f32[1,160]{1,0:T(1,128)S(1)}, f32[1,160]{1,0:T(1,128)}, u32[]{:S(2)}) copy-start(f32[1,160]{1,0:T(1,128)} %param.15) | copy-start | bytes 1924
  8.5 13.9 %copy-start.10 = (f32[1,160]{1,0:T(1,128)S(1)}, f32[1,160]{1,0:T(1,128)}, u32[]{:S(2)}) copy-start(f32[1,160]{1,0:T(1,128)} %param.16) | copy-start | bytes 1924
  8.5 42.8 %collective-permute-start.1 = (bf16[320,768]{1,0:T(8,128)(2,1)S(1)}, bf16[320,768]{1,0:T(8,128)(2,1)}, u32[]{:S(2)}, u32[]{:S(2)}) collective-permute-start(bf16[320,768]{1,0:T(8,128)(2,1)S(1)} %bitcast.46), channel_id=1, source_target_pairs={{0,2},{2,4},{4,6},{6,8},{8,10},{10,12},{12,14},{1,3},{3,5},{5,7},{... | collective-permute-start | bytes 1474568 | tf_op jit(solution)/shard_map/ppermute | solution.py:168
  14.6 36.8 %collective-permute-start.2 = (bf16[320,768]{1,0:T(8,128)(2,1)}, bf16[320,768]{1,0:T(8,128)(2,1)}, u32[]{:S(2)}, u32[]{:S(2)}) collective-permute-start(bf16[320,768]{1,0:T(8,128)(2,1)} %bitcast.16), channel_id=1, source_target_pairs={{2,0},{4,2},{6,4},{8,6},{10,8},{12,10},{14,12},{3,1},{5,3},{7,5},{... | collective-permute-start | bytes 1474568 | tf_op jit(solution)/shard_map/ppermute | solution.py:169
  23.3 26.9 %collective-permute-start.3 = (bf16[6,160,2]{1,2,0:T(2,128)(2,1)S(1)}, bf16[6,160,2]{1,2,0:T(2,128)(2,1)S(1)}, u32[]{:S(2)}, u32[]{:S(2)}) collective-permute-start(bf16[6,160,2]{1,2,0:T(2,128)(2,1)S(1)} %get-tuple-element.23), channel_id=1, source_target_pairs={{0,2},{2,4},{4,6},{6,8},{8,10},{10,12},{12,14},{1,3},{3,5},{5,7},{... | collective-permute-start | bytes 11528 | tf_op jit(solution)/shard_map/ppermute | solution.py:168
  27.9 22.3 %collective-permute-start.4 = (bf16[6,160,2]{1,2,0:T(2,128)(2,1)S(1)}, bf16[6,160,2]{1,2,0:T(2,128)(2,1)S(1)}, u32[]{:S(2)}, u32[]{:S(2)}) collective-permute-start(bf16[6,160,2]{1,2,0:T(2,128)(2,1)S(1)} %get-tuple-element.24), channel_id=1, source_target_pairs={{2,0},{4,2},{6,4},{8,6},{10,8},{12,10},{14,12},{3,1},{5,3},{7,5},{... | collective-permute-start | bytes 11528 | tf_op jit(solution)/shard_map/ppermute | solution.py:169
  51.3 26.2 %copy-start.7 = (s32[1,16,4]{1,2,0:T(4,128)S(1)}, s32[1,16,4]{1,2,0:T(4,128)}, u32[]{:S(2)}) copy-start(s32[1,16,4]{1,2,0:T(4,128)} %param.19) | copy-start | bytes 772
  51.3 26.9 %copy-start.6 = (bf16[1,8,160]{2,1,0:T(8,128)(2,1)S(1)}, bf16[1,8,160]{2,1,0:T(8,128)(2,1)}, u32[]{:S(2)}) copy-start(bf16[1,8,160]{2,1,0:T(8,128)(2,1)} %param.18) | copy-start | bytes 7684
  51.3 27.7 %copy-start.5 = (f32[1,16,4]{1,2,0:T(4,128)S(1)}, f32[1,16,4]{1,2,0:T(4,128)}, u32[]{:S(2)}) copy-start(f32[1,16,4]{1,2,0:T(4,128)} %param.20) | copy-start | bytes 772
  76.1 6.7 %collective-permute-start.5 = (bf16[16,8,768]{2,1,0:T(8,128)(2,1)}, bf16[16,8,768]{2,1,0:T(8,128)(2,1)S(1)}, u32[]{:S(2)}, u32[]{:S(2)}) collective-permute-start(bf16[16,8,768]{2,1,0:T(8,128)(2,1)} %get-tuple-element.12), channel_id=1, source_target_pairs={{0,16},{16,0},{1,17},{17,1},{2,18},{18,2},{3,19},{19,3},{4,20},{20... | collective-permute-start | bytes 589832 | tf_op jit(solution)/shard_map/ppermute | solution.py:250
  82.7 12.4 %copy-start.2 = (bf16[16,8,768]{2,1,0:T(8,128)(2,1)}, bf16[16,8,768]{2,1,0:T(8,128)(2,1)S(1)}, u32[]{:S(2)}) copy-start(bf16[16,8,768]{2,1,0:T(8,128)(2,1)S(1)} %collective-permute-done.5.mid_ref) | copy-start | bytes 589828
  82.7 7.4 %collective-permute-start.6 = (bf16[16,8,768]{2,1,0:T(8,128)(2,1)S(1)}, bf16[16,8,768]{2,1,0:T(8,128)(2,1)S(1)}, u32[]{:S(2)}, u32[]{:S(2)}) collective-permute-start(bf16[16,8,768]{2,1,0:T(8,128)(2,1)S(1)} %collective-permute-done.5.mid_ref), channel_id=1, source_target_pairs={{0,2},{2,4},{4,6},{6,8},{8,10},{10,12},{12,14},{1,3},{3,5},{5,7},{... | collective-permute-start | bytes 589832 | tf_op jit(solution)/shard_map/ppermute | solution.py:168
  87.0 8.1 %collective-permute-start.7 = (bf16[16,8,768]{2,1,0:T(8,128)(2,1)S(1)}, bf16[16,8,768]{2,1,0:T(8,128)(2,1)S(1)}, u32[]{:S(2)}, u32[]{:S(2)}) collective-permute-start(bf16[16,8,768]{2,1,0:T(8,128)(2,1)S(1)} %collective-permute-done.5.mid_ref), channel_id=1, source_target_pairs={{2,0},{4,2},{6,4},{8,6},{10,8},{12,10},{14,12},{3,1},{5,3},{7,5},{... | collective-permute-start | bytes 589832 | tf_op jit(solution)/shard_map/ppermute | solution.py:169
  90.2 4.9 %copy-start.3 = (bf16[16,8,768]{2,1,0:T(8,128)(2,1)}, bf16[16,8,768]{2,1,0:T(8,128)(2,1)S(1)}, u32[]{:S(2)}) copy-start(bf16[16,8,768]{2,1,0:T(8,128)(2,1)S(1)} %collective-permute-done.6.up_ref) | copy-start | bytes 589828
  95.1 0.7 copy-start.4
where the time goes:
time: 102 us
  Pallas kernels  50.6 us (50%)
  starting transfers between devices  20.1 us (20%)
  local copies, waits for them, and re-layouts  18.1 us (18%)
  waiting for transfers between devices  9.76 us (10%)
  other arithmetic  2.9 us (3%)
    pallas_call x1, Pallas kernels, on_device(): pl.pallas_call(second_kernel, name='conv_second', out_shape=(jax.ShapeDty...  24.7 us
    pallas_call x1, Pallas kernels, on_device(): pl.pallas_call(first_kernel, name='conv_first_inner', out_shape=(jax.Shap...  20 us
    ppermute x3, starting transfers between devices, both_ways(): lax.ppermute(tail, axis, [(i, i + 1) for i in range(n - 1)])  14 us
    pallas_call x1, Pallas kernels, on_device(): pl.pallas_call(third_kernel, name='exchange', grid=(rows // step,), out_s...  5.89 us
    slice x5, local copies, waits for them, and re-layouts, on_device(): own = jnp.stack([source[:, :, i] for i in (0, 1, width - 2, width - 1)])  4.96 us
    ppermute x3, waiting for transfers between devices, both_ways(): lax.ppermute(head, axis, [(i + 1, i) for i in range(n - 1)])  4.93 us
    ppermute x3, starting transfers between devices, both_ways(): lax.ppermute(head, axis, [(i + 1, i) for i in range(n - 1)])  4.04 us
    transpose x3, local copies, waits for them, and re-layouts, row_block(): return part.transpose(1, 0, 2).reshape(-1, width)  3.8 us
  transfers between devices with their start and end apart: 8, of which 3 were waited for; matrix products, arithmetic and copies ran while one was open for 15% of the time, Pallas kernels for 20%

commit v1 on v0

v1 whole, which is shorter than its diff:
```python
import functools

import jax
import jax.numpy as jnp
from jax import lax
from jax.experimental import pallas as pl
from jax.experimental.pallas import tpu as pltpu
from jax.sharding import PartitionSpec as P

F32 = jnp.float32
BF16 = jnp.bfloat16
LANES = 128
SIDE = 64
VMEM_LIMIT = 58 * 1024 * 1024


def lane_of(shape):
    return lax.broadcasted_iota(jnp.int32, shape, 1)


def stacked_rows(edge):
    return jnp.concatenate(
        [pltpu.roll(edge, 1, 1), edge, pltpu.roll(edge, LANES - 1, 1)], axis=0
    ).astype(BF16)


def edge_terms(weights, edge):
    ch = edge.shape[0]
    taps = jnp.dot(weights, stacked_rows(edge), preferred_element_type=F32)
    return jnp.where(lane_of((ch, LANES)) < SIDE, taps[:ch], taps[2 * ch :])


def conv_row(weights, rows3, edges, row, offset):
    ch, width = edges.shape[0], rows3.shape[1]
    taps = jnp.dot(weights, rows3, preferred_element_type=F32)
    at = lane_of((ch, LANES))
    left = jnp.sum(jnp.where(at == row + 2, edges, 0.0), axis=1, keepdims=True)
    right = jnp.sum(jnp.where(at == row + 2 + SIDE, edges, 0.0), axis=1, keepdims=True)
    lane = lane_of((ch, width))
    west = jnp.where(lane == 0, left, pltpu.roll(taps[:ch], 1, 1))
    east = jnp.where(lane == width - 1, right, pltpu.roll(taps[2 * ch :], width - 1, 1))
    return taps[ch : 2 * ch] + west + east + offset


def silu(u):
    return u / (1.0 + jnp.exp(-u))


def main_kernel(
    counts, x_ref, w1_ref, w2_ref, vec_ref, ex_ref,
    hid_ref, mid_ref, up_ref, down_ref,
    flat, x, hf, w1, w2, edges1, edges2, mine, far, own, face,
    row_send, row_recv, lon_send, lon_recv, mp_send, mp_recv, lat_send, lat_recv,
):
    ch, rows, width = x_ref.shape
    n_lat, chunks = counts
    lat = lax.axis_index("lat")
    has_up, has_down = lat > 0, lat < n_lat - 1
    above, below = {"lat": lat - 1}, {"lat": lat + 1}
    beside = {"lon": 1 - lax.axis_index("lon")}
    partner = {"mp": 1 - lax.axis_index("mp")}
    MESH = pl.DeviceIdType.MESH

    barrier = pltpu.get_barrier_semaphore()
    pl.semaphore_signal(barrier, inc=1, device_id=beside, device_id_type=MESH)
    pl.semaphore_signal(barrier, inc=1, device_id=partner, device_id_type=MESH)

    @pl.when(has_up)
    def _():
        pl.semaphore_signal(barrier, inc=1, device_id=above, device_id_type=MESH)

    @pl.when(has_down)
    def _():
        pl.semaphore_signal(barrier, inc=1, device_id=below, device_id_type=MESH)

    for j in range(width // LANES):
        flat[j] = x_ref[:, :, j * LANES : (j + 1) * LANES].astype(F32).reshape(ch * rows, LANES)
    for r in range(rows):
        for j in range(width // LANES):
            x[(r + 2) * ch : (r + 3) * ch, j * LANES : (j + 1) * LANES] = flat.at[j][
                pl.ds(r, ch, stride=rows), :
            ].astype(BF16)

    pl.semaphore_wait(barrier, 2 + has_up.astype(jnp.int32) + has_down.astype(jnp.int32))

    def copy(src, dst, send, recv, where):
        return pltpu.make_async_remote_copy(
            src_ref=src, dst_ref=dst, send_sem=send, recv_sem=recv,
            device_id=where, device_id_type=MESH,
        )

    two = 2 * ch
    to_up = copy(
        x.at[pl.ds(two, two)], x.at[pl.ds((rows + 2) * ch, two)],
        row_send.at[0], row_recv.at[0], above,
    )
    to_down = copy(
        x.at[pl.ds(rows * ch, two)], x.at[pl.ds(0, two)],
        row_send.at[1], row_recv.at[1], below,
    )

    @pl.when(has_up)
    def _():
        to_up.start()

    @pl.when(has_down)
    def _():
        to_down.start()

    at = lane_of((ch, LANES))

    def columns(row_list, n):
        zero = jnp.zeros((ch, LANES), F32)
        sent = [zero, zero, zero]
        kept = [zero, zero]
        if n:
            sent = [mine[0, k * ch : (k + 1) * ch] for k in range(3)]
            kept = [own[k * ch : (k + 1) * ch] for k in range(2)]
        for r in row_list:
            here = pl.ds((r + 2) * ch, ch)
            first = x[here, :LANES].astype(F32)
            last = x[here, width - LANES :].astype(F32)
            left, right = at == r + 2, at == r + 2 + SIDE
            sent[0] = jnp.where(left, last[:, LANES - 2 : LANES - 1], sent[0])
            sent[1] = jnp.where(left, last[:, LANES - 1 :], sent[1])
            sent[1] = jnp.where(right, first[:, :1], sent[1])
            sent[2] = jnp.where(right, first[:, 1:2], sent[2])
            kept[0] = jnp.where(right, last[:, LANES - 1 :], kept[0])
            kept[1] = jnp.where(left, first[:, :1], kept[1])
        for k in range(3):
            mine[n, k * ch : (k + 1) * ch] = sent[k]
        for k in range(2):
            own[k * ch : (k + 1) * ch] = kept[k]
        return copy(mine.at[n], far.at[n], lon_send.at[n], lon_recv.at[n], beside)

    lon0 = columns(range(rows), 0)
    lon0.start()

    def taps(src, dst):
        for c in range(3):
            block = jnp.concatenate([src[a, c].astype(F32) for a in range(3)], axis=0)
            dst[c * ch : (c + 1) * ch] = block.T.astype(BF16)

    taps(w1_ref, w1)
    taps(w2_ref, w2)
    b1, b2, gain = vec_ref[:, 0:1], vec_ref[:, 1:2], vec_ref[:, 2:3]
    lon0.wait()
    edges1[...] = edge_terms(w1[...], far[0, ch : 2 * ch])

    def first(r):
        rows3 = x[pl.ds(pl.multiple_of((r + 1) * ch, 16), 3 * ch), :]
        return silu(conv_row(w1[...], rows3, edges1[...], r, vec_ref[:, 0:1])).astype(BF16)

    split = rows - 4

    @pl.loop(1, split)
    def _(r):
        hf[pl.ds(pl.multiple_of((r + 1) * ch, 16), ch), :] = first(r)

    @pl.when(has_up)
    def _():
        to_up.wait_send()
        to_down.wait_recv()

    @pl.when(has_down)
    def _():
        to_down.wait_send()
        to_up.wait_recv()

    @pl.when(jnp.logical_not(has_up))
    def _():
        x[:two] = jnp.zeros((two, width), BF16)

    @pl.when(jnp.logical_not(has_down))
    def _():
        x[(rows + 2) * ch :] = jnp.zeros((two, width), BF16)

    lon1 = columns((-2, -1, rows, rows + 1), 1)
    lon1.start()

    @pl.loop(split, rows - 1)
    def _(r):
        hf[pl.ds(pl.multiple_of((r + 1) * ch, 16), ch), :] = first(r)

    lon1.wait()
    edges1[...] = edge_terms(w1[...], far[1, ch : 2 * ch])

    @pl.loop(0, 4)
    def _(q):
        r = jnp.where(q < 2, q - 1, rows + q - 3)
        hf[pl.ds(pl.multiple_of((r + 1) * ch, 16), ch), :] = first(r)

    @pl.when(jnp.logical_not(has_up))
    def _():
        hf[:ch] = jnp.zeros((ch, width), BF16)

    @pl.when(jnp.logical_not(has_down))
    def _():
        hf[(rows + 1) * ch :] = jnp.zeros((ch, width), BF16)

    column = None
    for k in range(3):
        edge = far[1, k * ch : (k + 1) * ch]
        if k != 1:
            edge = edge + own[(k // 2) * ch : (k // 2 + 1) * ch]
        term = jnp.dot(
            w1[k * ch : (k + 1) * ch], stacked_rows(edge), preferred_element_type=F32
        )
        column = term if column is None else column + term
    column = silu(column + b1)
    lane = jnp.where(at >= SIDE, at - SIDE, at)
    lowest = jnp.where(has_up, 1, 2)
    highest = jnp.where(has_down, rows + 2, rows + 1)
    column = jnp.where((lane < lowest) | (lane > highest), 0.0, column)
    edges2[...] = edge_terms(w2[...], column.astype(BF16).astype(F32))

    size = rows // chunks
    to_partner = []
    for n in range(chunks):
        part = pl.ds(n * size, size)
        to_partner.append(copy(face.at[part], mid_ref.at[part], mp_send.at[n], mp_recv.at[n], partner))
    face_up, face_down = [], []
    for n in range(chunks):
        part = pl.ds(n * size, size)
        face_up.append(copy(mid_ref.at[part], down_ref.at[part], lat_send.at[0, n], lat_recv.at[0, n], above))
        face_down.append(copy(mid_ref.at[part], up_ref.at[part], lat_send.at[1, n], lat_recv.at[1, n], below))

    def forward(n):
        to_partner[n].wait()

        @pl.when(has_up)
        def _():
            face_up[n].start()

        @pl.when(has_down)
        def _():
            face_down[n].start()

    for n in range(chunks):

        @pl.loop(n * size, (n + 1) * size)
        def _(r):
            here = pl.ds(pl.multiple_of(r * ch, 16), ch)
            rows3 = hf[pl.ds(pl.multiple_of(r * ch, 16), 3 * ch), :]
            u = conv_row(w2[...], rows3, edges2[...], r, vec_ref[:, 1:2])
            u = u + x[pl.ds(pl.multiple_of((r + 2) * ch, 16), ch), :].astype(F32)
            mean = jnp.sum(u * u, axis=0, keepdims=True) * (1.0 / ch)
            h = (u * lax.rsqrt(mean + 1e-06) * vec_ref[:, 2:3]).astype(BF16)
            hid_ref[here, :] = h
            face[r] = jnp.dot(ex_ref[...], h, preferred_element_type=F32).astype(BF16)

        to_partner[n].start()
        if n:
            forward(n - 1)
    forward(chunks - 1)

    @pl.when(has_up)
    def _():
        for n in range(chunks):
            face_up[n].wait_send()
            face_down[n].wait_recv()

    @pl.when(has_down)
    def _():
        for n in range(chunks):
            face_down[n].wait_send()
            face_up[n].wait_recv()

    @pl.when(jnp.logical_not(has_up))
    def _():
        up_ref[...] = jnp.zeros(up_ref.shape, BF16)

    @pl.when(jnp.logical_not(has_down))
    def _():
        down_ref[...] = jnp.zeros(down_ref.shape, BF16)


def third_kernel(
    rows_ref, weights_ref, hid_ref, up_ref, mid_ref, down_ref, im_ref, mask_ref, out_ref, band, flat
):
    ch, step, width = out_ref.shape
    rows = up_ref.shape[0]
    base = pl.program_id(0) * step
    band[:rows] = up_ref[...].astype(F32)
    band[rows : 2 * rows] = mid_ref[...].astype(F32)
    band[2 * rows :] = down_ref[...].astype(F32)
    for d in range(step):
        total = None
        for k in range(rows_ref.shape[1]):
            term = weights_ref[base + d, k] * band[rows_ref[base + d, k]]
            total = term if total is None else total + term
        mixed = jnp.dot(im_ref[...], total.astype(BF16), preferred_element_type=F32)
        h = hid_ref[d * ch : (d + 1) * ch, :].astype(F32)
        value = h + mask_ref[d : d + 1, :].astype(F32) * mixed
        for j in range(width // LANES):
            flat.at[j][pl.ds(d, ch, stride=step), :] = value[:, j * LANES : (j + 1) * LANES]
    for j in range(width // LANES):
        out_ref[:, :, j * LANES : (j + 1) * LANES] = (
            flat[j].reshape(ch, step, LANES).astype(BF16)
        )


def vmem():
    return pl.BlockSpec(memory_space=pltpu.VMEM)


def smem():
    return pl.BlockSpec(memory_space=pltpu.SMEM)


def params():
    return pltpu.CompilerParams(vmem_limit_bytes=VMEM_LIMIT)


def on_device(
    state, conv_first, bias_first, conv_second, bias_second, norm_gain, export_weight,
    import_weight, regrid_rows, regrid_weights, sea_mask,
):
    source = state[0]
    ch, rows, width = source.shape
    lat = lax.axis_index("lat")
    n_lat = lax.axis_size("lat")

    vectors = jnp.stack([bias_first[0], bias_second[0], norm_gain[0]], axis=1)
    n_face = export_weight.shape[2]
    chunks = 4
    fields = jax.ShapeDtypeStruct((rows, n_face, width), BF16)
    dma = pltpu.SemaphoreType.DMA
    hidden, mid, up, down = pl.pallas_call(
        functools.partial(main_kernel, (n_lat, chunks)),
        name="convolutions",
        out_shape=(jax.ShapeDtypeStruct((rows * ch, width), BF16), fields, fields, fields),
        in_specs=[vmem()] * 5,
        out_specs=(vmem(),) * 4,
        scratch_shapes=[
            pltpu.VMEM((width // LANES, rows * ch, LANES), F32),
            pltpu.VMEM(((rows + 4) * ch, width), BF16),
            pltpu.VMEM(((rows + 2) * ch, width), BF16),
            pltpu.VMEM((3 * ch, 3 * ch), BF16),
            pltpu.VMEM((3 * ch, 3 * ch), BF16),
            pltpu.VMEM((ch, LANES), F32),
            pltpu.VMEM((ch, LANES), F32),
            pltpu.VMEM((2, 3 * ch, LANES), F32),
            pltpu.VMEM((2, 3 * ch, LANES), F32),
            pltpu.VMEM((2 * ch, LANES), F32),
            pltpu.VMEM((rows, n_face, width), BF16),
            dma((2,)), dma((2,)), dma((2,)), dma((2,)),
            dma((chunks,)), dma((chunks,)), dma((2, chunks)), dma((2, chunks)),
        ],
        compiler_params=pltpu.CompilerParams(
            vmem_limit_bytes=VMEM_LIMIT, collective_id=0, has_side_effects=True
        ),
    )(source, conv_first[0], conv_second[0], vectors, export_weight[0].T)

    weights = regrid_weights[0]
    normed = weights / jnp.sum(weights, axis=1, keepdims=True)
    local_rows = regrid_rows[0] - (lat - 1) * rows

    step = 8
    whole = lambda shape: pl.BlockSpec(shape, lambda i: (0,) * len(shape))
    out = pl.pallas_call(
        third_kernel,
        name="exchange",
        grid=(rows // step,),
        out_shape=jax.ShapeDtypeStruct((ch, rows, width), BF16),
        in_specs=[
            smem(),
            smem(),
            pl.BlockSpec((step * ch, width), lambda i: (i, 0)),
            whole(mid.shape),
            whole(mid.shape),
            whole(mid.shape),
            whole((ch, n_face)),
            pl.BlockSpec((step, width), lambda i: (i, 0)),
        ],
        out_specs=pl.BlockSpec((ch, step, width), lambda i: (0, i, 0)),
        scratch_shapes=[
            pltpu.VMEM((3 * rows, n_face, width), F32),
            pltpu.VMEM((width // LANES, step * ch, LANES), F32),
        ],
        compiler_params=params(),
    )(local_rows, normed, hidden, up, mid, down, import_weight[0].T, sea_mask[0])
    return out[None]


def solution(mesh):
    return jax.shard_map(
        on_device,
        mesh=mesh,
        in_specs=(
            P("mp", None, "lat", "lon"),
            P("mp", None, None, None, None),
            P("mp", None),
            P("mp", None, None, None, None),
            P("mp", None),
            P("mp", None),
            P("mp", None, None),
            P("mp", None, None),
            P("mp", "lat", None),
            P("mp", "lat", None),
            P("mp", "lat", "lon"),
        ),
        out_specs=P("mp", None, "lat", "lon"),
        check_vma=False,
    )
```

time: 102 us -> 74.3 us (0.73)
  starting transfers between devices: 20.1 us -> 0 us
  Pallas kernels: 50.6 us -> 67.7 us
  local copies, waits for them, and re-layouts: 18.1 us -> 3.6 us
  waiting for transfers between devices: 9.76 us -> 0 us
    ppermute x8 -> x0, starting transfers between devices: 20.1 us -> none  [the longest x3 14 us: both_ways(): lax.ppermute(tail, axis, [(i, i + 1) for i in range(n - 1)])]
    pallas_call x2 -> x1, Pallas kernels: 44.7 us -> 61.8 us  [on_device(): pl.pallas_call(functools.partial(main_kernel, (n_lat, chunks)), name='con...]
    ppermute x8 -> x0, waiting for transfers between devices: 9.76 us -> none  [the longest x3 4.93 us: both_ways(): lax.ppermute(head, axis, [(i + 1, i) for i in range(n - 1)])]
    transpose x5 -> x0, local copies, waits for them, and re-layouts: 5.63 us -> none  [the longest x3 3.8 us: row_block(): return part.transpose(1, 0, 2).reshape(-1, width)]
    slice x9 -> x0, local copies, waits for them, and re-layouts: 5.16 us -> none  [the longest x5 4.96 us: on_device(): own = jnp.stack([source[:, :, i] for i in (0, 1, width - 2, width - 1)])]
    reshape x2 -> x0, local copies, waits for them, and re-layouts: 2.52 us -> none  [taps(): return kernel.transpose(1, 3, 0, 2).reshape(3 * ch, 3 * ch)]
    another operation x3 -> x1, local copies, waits for them, and re-layouts: 2.24 us -> 0.75 us  [on_device(): vectors = jnp.stack([bias_first[0], bias_second[0], norm_gain[0]], axis=1)]
    convert_element_type x2 -> x0, other arithmetic: 1.32 us -> none  [the longest x1 0.73 us: in_lanes(): jnp.concatenate([cols[:3], cols[3:]], axis=2).reshape(3 * ch, LANES)]
  transfers between devices with their start and end apart: 8 -> 0, of which waited for: 3 -> 0; matrix products, arithmetic and copies ran while one was open for 15% -> 0% of each run, Pallas kernels for 20% -> 0%
where the time goes in v1:
time: 74.3 us; the launch traced here: 74.1 us
  Pallas kernels  67.7 us (91%)
  local copies, waits for them, and re-layouts  3.6 us (5%)
  other arithmetic  2.77 us (4%)
    pallas_call x1, Pallas kernels, on_device(): pl.pallas_call(functools.partial(main_kernel, (n_lat, chunks)), name='con...  61.8 us
    pallas_call x1, Pallas kernels, on_device(): pl.pallas_call(third_kernel, name='exchange', grid=(rows // step,), out_s...  5.93 us

profile of v1, /device:TPU:0, one launch (start us, length us, event | category | flops | bytes accessed | tf_op | source)
XLA Modules:
  0.0 74.1 jit_solution(10584093416994060706)
XLA Ops:
  0.0 0.7 reduce_sum.9
  0.7 0.7 subtract_bitcast_fusion
  1.4 0.7 pad_maximum_fusion
  2.1 0.7 copy.29.rows_ref
  2.8 0.8 %copy.25 = f32[16,4]{1,0:T(8,128)S(1)} copy(f32[16,4]{0,1:T(4,128)} %bitcast.22) | data formatting | bytes 512 | tf_op jit(solution)/shard_map/squeeze | solution.py:355
  3.5 0.7 broadcast_divide_fusion.weights_ref
  4.2 1.4 %copy.28 = bf16[1,8,160]{1,2,0:T(8,128)(2,1)} copy(bf16[1,8,160]{2,1,0:T(8,128)(2,1)} %param.18) | data formatting | bytes 5120 | tf_op args[7]
  5.6 0.8 %copy.27.vec_ref = f32[160,3]{1,0:T(8,128)} copy(f32[160,3]{0,1:T(4,128)S(1)} %pad_maximum_fusion) | data formatting | bytes 3840 | tf_op jit(solution)/shard_map/stack | solution.py:324
  6.4 61.8 %convolutions.1 = (bf16[2560,768]{1,0:T(8,128)(2,1)}, bf16[16,8,768]{2,1,0:T(8,128)(2,1)}, bf16[16,8,768]{2,1,0:T(8,128)(2,1)}, bf16[16,8,768]{2,1,0:T(8,128)(2,1)}) custom-call(bf16[160,16,768]{2,1,0:T(8,128)(2,1)} %bitcast.17, bf16[3,3,160,160]{3,2,1,0:T(8,128)(2,1)} %bitcast.18, bf16[3,3,160,160]{3,2,1,0:T(8,128)(2,1)} %bitcast.19, ...), custom_call_target="tpu_custom_call" | custom-call | tf_op jit(solution)/shard_map/convolutions/pallas_call | solution.py:329
  68.1 5.9 %exchange.1 = bf16[160,16,768]{2,1,0:T(8,128)(2,1)} custom-call(s32[16,4]{1,0:T(8,128)} %copy.29.rows_ref, f32[16,4]{1,0:T(8,128)} %broadcast_divide_fusion.weights_ref, bf16[2560,768]{1,0:T(8,128)(2,1)} %get-tuple-element.9.hid_ref, bf16[16,8,768]{2,1,0:T(8,128)(2,1)} %get-tuple-element.10.up_ref, bf16[16,8,768]{2,1,0:T(8,128)(2,1)} %get-tuple-element.11.mid_ref, ...), custom_call_target="tpu_custom_call" | custom-call | tf_op jit(solution)/shard_map/exchange/pallas_call | solution.py:361

commit v2 on v1

--- a/solution.py
+++ b/solution.py
@@ -33,17 +33,22 @@
 def conv_row(weights, rows3, edges, row, offset):
     ch, width = edges.shape[0], rows3.shape[1]
     taps = jnp.dot(weights, rows3, preferred_element_type=F32)
-    at = lane_of((ch, LANES))
-    left = jnp.sum(jnp.where(at == row + 2, edges, 0.0), axis=1, keepdims=True)
-    right = jnp.sum(jnp.where(at == row + 2 + SIDE, edges, 0.0), axis=1, keepdims=True)
-    lane = lane_of((ch, width))
-    west = jnp.where(lane == 0, left, pltpu.roll(taps[:ch], 1, 1))
-    east = jnp.where(lane == width - 1, right, pltpu.roll(taps[2 * ch :], width - 1, 1))
+    lane = lane_of((ch, LANES))
+    left = pltpu.roll(edges, LANES - 2 - row, 1)
+    right = pltpu.roll(edges, LANES - 1 - (row + 2 + SIDE), 1)
+    west = pltpu.roll(taps[:ch], 1, 1)
+    west = jnp.concatenate([jnp.where(lane == 0, left, west[:, :LANES]), west[:, LANES:]], axis=1)
+    east = pltpu.roll(taps[2 * ch :], width - 1, 1)
+    east = jnp.concatenate(
+        [east[:, : width - LANES], jnp.where(lane == LANES - 1, right, east[:, width - LANES :])],
+        axis=1,
+    )
     return taps[ch : 2 * ch] + west + east + offset
 
 
 def silu(u):
-    return u / (1.0 + jnp.exp(-u))
+    half = 0.5 * u
+    return half + half * jnp.tanh(half)
 
 
 def main_kernel(
@@ -151,77 +156,36 @@
         rows3 = x[pl.ds(pl.multiple_of((r + 1) * ch, 16), 3 * ch), :]
         return silu(conv_row(w1[...], rows3, edges1[...], r, vec_ref[:, 0:1])).astype(BF16)
 
-    split = rows - 4
-
-    @pl.loop(1, split)
+    @pl.loop(1, rows - 1)
     def _(r):
         hf[pl.ds(pl.multiple_of((r + 1) * ch, 16), ch), :] = first(r)
 
-    @pl.when(has_up)
-    def _():
-        to_up.wait_send()
-        to_down.wait_recv()
-
-    @pl.when(has_down)
-    def _():
-        to_down.wait_send()
-        to_up.wait_recv()
-
-    @pl.when(jnp.logical_not(has_up))
-    def _():
-        x[:two] = jnp.zeros((two, width), BF16)
-
-    @pl.when(jnp.logical_not(has_down))
-    def _():
-        x[(rows + 2) * ch :] = jnp.zeros((two, width), BF16)
-
-    lon1 = columns((-2, -1, rows, rows + 1), 1)
-    lon1.start()
-
-    @pl.loop(split, rows - 1)
-    def _(r):
-        hf[pl.ds(pl.multiple_of((r + 1) * ch, 16), ch), :] = first(r)
-
-    lon1.wait()
-    edges1[...] = edge_terms(w1[...], far[1, ch : 2 * ch])
-
-    @pl.loop(0, 4)
-    def _(q):
-        r = jnp.where(q < 2, q - 1, rows + q - 3)
-        hf[pl.ds(pl.multiple_of((r + 1) * ch, 16), ch), :] = first(r)
-
-    @pl.when(jnp.logical_not(has_up))
-    def _():
-        hf[:ch] = jnp.zeros((ch, width), BF16)
-
-    @pl.when(jnp.logical_not(has_down))
-    def _():
-        hf[(rows + 1) * ch :] = jnp.zeros((ch, width), BF16)
-
-    column = None
-    for k in range(3):
-        edge = far[1, k * ch : (k + 1) * ch]
-        if k != 1:
-            edge = edge + own[(k // 2) * ch : (k // 2 + 1) * ch]
-        term = jnp.dot(
-            w1[k * ch : (k + 1) * ch], stacked_rows(edge), preferred_element_type=F32
-        )
-        column = term if column is None else column + term
-    column = silu(column + b1)
-    lane = jnp.where(at >= SIDE, at - SIDE, at)
-    lowest = jnp.where(has_up, 1, 2)
-    highest = jnp.where(has_down, rows + 2, rows + 1)
-    column = jnp.where((lane < lowest) | (lane > highest), 0.0, column)
-    edges2[...] = edge_terms(w2[...], column.astype(BF16).astype(F32))
-
-    size = rows // chunks
+    def column_terms(n):
+        column = None
+        for k in range(3):
+            edge = far[n, k * ch : (k + 1) * ch]
+            if k != 1:
+                edge = edge + own[(k // 2) * ch : (k // 2 + 1) * ch]
+            term = jnp.dot(
+                w1[k * ch : (k + 1) * ch], stacked_rows(edge), preferred_element_type=F32
+            )
+            column = term if column is None else column + term
+        column = silu(column + b1)
+        lane = jnp.where(at >= SIDE, at - SIDE, at)
+        lowest = jnp.where(has_up, 1, 2)
+        highest = jnp.where(has_down, rows + 2, rows + 1)
+        column = jnp.where((lane < lowest) | (lane > highest), 0.0, column)
+        edges2[...] = edge_terms(w2[...], column.astype(BF16).astype(F32))
+
+    third = (rows - 4) // 3
+    parts = [(2 + n * third, third) for n in range(3)] + [(0, 2), (rows - 2, 2)]
     to_partner = []
     for n in range(chunks):
-        part = pl.ds(n * size, size)
+        part = pl.ds(*parts[n])
         to_partner.append(copy(face.at[part], mid_ref.at[part], mp_send.at[n], mp_recv.at[n], partner))
     face_up, face_down = [], []
     for n in range(chunks):
-        part = pl.ds(n * size, size)
+        part = pl.ds(*parts[n])
         face_up.append(copy(mid_ref.at[part], down_ref.at[part], lat_send.at[0, n], lat_recv.at[0, n], above))
         face_down.append(copy(mid_ref.at[part], up_ref.at[part], lat_send.at[1, n], lat_recv.at[1, n], below))
 
@@ -236,9 +200,8 @@
         def _():
             face_down[n].start()
 
-    for n in range(chunks):
-
-        @pl.loop(n * size, (n + 1) * size)
+    def finish(n):
+        @pl.loop(parts[n][0], sum(parts[n]))
         def _(r):
             here = pl.ds(pl.multiple_of(r * ch, 16), ch)
             rows3 = hf[pl.ds(pl.multiple_of(r * ch, 16), 3 * ch), :]
@@ -250,9 +213,56 @@
             face[r] = jnp.dot(ex_ref[...], h, preferred_element_type=F32).astype(BF16)
 
         to_partner[n].start()
-        if n:
-            forward(n - 1)
-    forward(chunks - 1)
+
+    column_terms(0)
+    finish(0)
+    finish(1)
+    forward(0)
+    finish(2)
+    forward(1)
+
+    @pl.when(has_up)
+    def _():
+        to_up.wait_send()
+        to_down.wait_recv()
+
+    @pl.when(has_down)
+    def _():
+        to_down.wait_send()
+        to_up.wait_recv()
+
+    @pl.when(jnp.logical_not(has_up))
+    def _():
+        x[:two] = jnp.zeros((two, width), BF16)
+
+    @pl.when(jnp.logical_not(has_down))
+    def _():
+        x[(rows + 2) * ch :] = jnp.zeros((two, width), BF16)
+
+    lon1 = columns((-2, -1, rows, rows + 1), 1)
+    lon1.start()
+    forward(2)
+    lon1.wait()
+    edges1[...] = edge_terms(w1[...], far[1, ch : 2 * ch])
+
+    @pl.loop(0, 4)
+    def _(q):
+        r = jnp.where(q < 2, q - 1, rows + q - 3)
+        hf[pl.ds(pl.multiple_of((r + 1) * ch, 16), ch), :] = first(r)
+
+    @pl.when(jnp.logical_not(has_up))
+    def _():
+        hf[:ch] = jnp.zeros((ch, width), BF16)
+
+    @pl.when(jnp.logical_not(has_down))
+    def _():
+        hf[(rows + 1) * ch :] = jnp.zeros((ch, width), BF16)
+
+    column_terms(1)
+    finish(3)
+    finish(4)
+    forward(3)
+    forward(4)
 
     @pl.when(has_up)
     def _():
@@ -281,14 +291,19 @@
     ch, step, width = out_ref.shape
     rows = up_ref.shape[0]
     base = pl.program_id(0) * step
+    start = (lax.axis_index("lat") - 1) * rows
     band[:rows] = up_ref[...].astype(F32)
     band[rows : 2 * rows] = mid_ref[...].astype(F32)
     band[2 * rows :] = down_ref[...].astype(F32)
     for d in range(step):
         total = None
         for k in range(rows_ref.shape[1]):
-            term = weights_ref[base + d, k] * band[rows_ref[base + d, k]]
+            weight = weights_ref[base + d, k]
+            at = jnp.clip(rows_ref[base + d, k] - start, 0, 3 * rows - 1)
+            term = weight * band[at]
             total = term if total is None else total + term
+            weight_sum = weight if k == 0 else weight_sum + weight
+        total = total / jnp.full(total.shape, weight_sum, F32)
         mixed = jnp.dot(im_ref[...], total.astype(BF16), preferred_element_type=F32)
         h = hid_ref[d * ch : (d + 1) * ch, :].astype(F32)
         value = h + mask_ref[d : d + 1, :].astype(F32) * mixed
@@ -318,12 +333,11 @@
 ):
     source = state[0]
     ch, rows, width = source.shape
-    lat = lax.axis_index("lat")
     n_lat = lax.axis_size("lat")
 
     vectors = jnp.stack([bias_first[0], bias_second[0], norm_gain[0]], axis=1)
     n_face = export_weight.shape[2]
-    chunks = 4
+    chunks = 5
     fields = jax.ShapeDtypeStruct((rows, n_face, width), BF16)
     dma = pltpu.SemaphoreType.DMA
     hidden, mid, up, down = pl.pallas_call(
@@ -352,10 +366,6 @@
         ),
     )(source, conv_first[0], conv_second[0], vectors, export_weight[0].T)
 
-    weights = regrid_weights[0]
-    normed = weights / jnp.sum(weights, axis=1, keepdims=True)
-    local_rows = regrid_rows[0] - (lat - 1) * rows
-
     step = 8
     whole = lambda shape: pl.BlockSpec(shape, lambda i: (0,) * len(shape))
     out = pl.pallas_call(
@@ -379,7 +389,7 @@
             pltpu.VMEM((width // LANES, step * ch, LANES), F32),
         ],
         compiler_params=params(),
-    )(local_rows, normed, hidden, up, mid, down, import_weight[0].T, sea_mask[0])
+    )(regrid_rows[0], regrid_weights[0], hidden, up, mid, down, import_weight[0].T, sea_mask[0])
     return out[None]
 
 

time: 74.3 us -> 63.6 us (0.86)
  Pallas kernels: 67.7 us -> 57.8 us
  other arithmetic: 2.77 us -> 0.72 us
  local copies, waits for them, and re-layouts: 3.6 us -> 4.87 us
    pallas_call x1, Pallas kernels: 61.8 us -> 51.8 us  [on_device(): pl.pallas_call(functools.partial(main_kernel, (n_lat, chunks)), name='con...]
    squeeze x1 -> x2, local copies, waits for them, and re-layouts: 0.76 us -> 2.7 us  [the longest x1 1.35 us: on_device(): regrid_weights[0]]
where the time goes in v2:
time: 63.6 us; the launch traced here: 63.4 us
  Pallas kernels  57.8 us (91%)
  local copies, waits for them, and re-layouts  4.87 us (8%)
  other arithmetic  0.72 us (1%)
    pallas_call x1, Pallas kernels, on_device(): pl.pallas_call(functools.partial(main_kernel, (n_lat, chunks)), name='con...  51.8 us
    pallas_call x1, Pallas kernels, on_device(): pl.pallas_call(third_kernel, name='exchange', grid=(rows // step,), out_s...  5.95 us
    unnamed x1, local copies, waits for them, and re-layouts  1.41 us
    squeeze x1, local copies, waits for them, and re-layouts, on_device(): regrid_weights[0]  1.35 us
    squeeze x1, local copies, waits for them, and re-layouts, on_device(): regrid_rows[0]  1.35 us

profile of v2, /device:TPU:0, one launch (start us, length us, event | category | flops | bytes accessed | tf_op | source)
XLA Modules:
  0.0 63.4 jit_solution(8426197455428465285)
XLA Ops:
  0.0 0.7 %pad_maximum_fusion = f32[160,3]{0,1:T(4,128)S(1)} fusion(f32[160,1]{0,1:T(1,128)} %bitcast.24, f32[160,1]{0,1:T(1,128)} %bitcast.25, f32[160,1]{0,1:T(1,128)} %bitcast.26), kind=kLoop, calls=%fused_computation | loop fusion | flops 960 | bytes 3840 | tf_op jit(solution)/shard_map/stack | solution.py:338
  0.7 1.4 %copy.23.rows_ref = s32[16,4]{1,0:T(8,128)} copy(s32[16,4]{0,1:T(4,128)} %bitcast.22) | data formatting | bytes 512 | tf_op jit(solution)/shard_map/squeeze | solution.py:392
  2.1 1.4 %copy.24.weights_ref = f32[16,4]{1,0:T(8,128)} copy(f32[16,4]{0,1:T(4,128)} %bitcast.23) | data formatting | bytes 512 | tf_op jit(solution)/shard_map/squeeze | solution.py:392
  3.4 1.4 %copy.22 = bf16[1,8,160]{1,2,0:T(8,128)(2,1)} copy(bf16[1,8,160]{2,1,0:T(8,128)(2,1)} %param.18) | data formatting | bytes 5120 | tf_op args[7]
  4.8 0.8 %copy.21.vec_ref = f32[160,3]{1,0:T(8,128)} copy(f32[160,3]{0,1:T(4,128)S(1)} %pad_maximum_fusion) | data formatting | bytes 3840 | tf_op jit(solution)/shard_map/stack | solution.py:338
  5.6 51.8 %convolutions.1 = (bf16[2560,768]{1,0:T(8,128)(2,1)}, bf16[16,8,768]{2,1,0:T(8,128)(2,1)}, bf16[16,8,768]{2,1,0:T(8,128)(2,1)}, bf16[16,8,768]{2,1,0:T(8,128)(2,1)}) custom-call(bf16[160,16,768]{2,1,0:T(8,128)(2,1)} %bitcast.16, bf16[3,3,160,160]{3,2,1,0:T(8,128)(2,1)} %bitcast.17, bf16[3,3,160,160]{3,2,1,0:T(8,128)(2,1)} %bitcast.18, ...), custom_call_target="tpu_custom_call" | custom-call | tf_op jit(solution)/shard_map/convolutions/pallas_call | solution.py:343
  57.4 5.9 %exchange.1 = bf16[160,16,768]{2,1,0:T(8,128)(2,1)} custom-call(s32[16,4]{1,0:T(8,128)} %copy.23.rows_ref, f32[16,4]{1,0:T(8,128)} %copy.24.weights_ref, bf16[2560,768]{1,0:T(8,128)(2,1)} %get-tuple-element.9.hid_ref, bf16[16,8,768]{2,1,0:T(8,128)(2,1)} %get-tuple-element.10.up_ref, bf16[16,8,768]{2,1,0:T(8,128)(2,1)} %get-tuple-element.11.mid_ref, ...), custom_call_target="tpu_custom_call" | custom-call | tf_op jit(solution)/shard_map/exchange/pallas_call | solution.py:371

commit v3 on v2

--- a/solution.py
+++ b/solution.py
@@ -80,12 +80,14 @@
 
     for j in range(width // LANES):
         flat[j] = x_ref[:, :, j * LANES : (j + 1) * LANES].astype(F32).reshape(ch * rows, LANES)
-    for r in range(rows):
-        for j in range(width // LANES):
-            x[(r + 2) * ch : (r + 3) * ch, j * LANES : (j + 1) * LANES] = flat.at[j][
-                pl.ds(r, ch, stride=rows), :
-            ].astype(BF16)
-
+    def lay_out(row_list):
+        for r in row_list:
+            for j in range(width // LANES):
+                x[(r + 2) * ch : (r + 3) * ch, j * LANES : (j + 1) * LANES] = flat.at[j][
+                    pl.ds(r, ch, stride=rows), :
+                ].astype(BF16)
+
+    lay_out((0, 1, rows - 2, rows - 1))
     pl.semaphore_wait(barrier, 2 + has_up.astype(jnp.int32) + has_down.astype(jnp.int32))
 
     def copy(src, dst, send, recv, where):
@@ -112,6 +114,7 @@
     def _():
         to_down.start()
 
+    lay_out(range(2, rows - 2))
     at = lane_of((ch, LANES))
 
     def columns(row_list, n):

time: 63.6 us -> 63.2 us (level)
  no operation moved by 1% of the time
where the time goes in v3:
time: 63.2 us; the launch traced here: 62.9 us
  Pallas kernels  57.3 us (91%)
  local copies, waits for them, and re-layouts  4.87 us (8%)
  other arithmetic  0.72 us (1%)
    pallas_call x1, Pallas kernels, on_device(): pl.pallas_call(functools.partial(main_kernel, (n_lat, chunks)), name='con...  51.4 us
    pallas_call x1, Pallas kernels, on_device(): pl.pallas_call(third_kernel, name='exchange', grid=(rows // step,), out_s...  5.95 us
    unnamed x1, local copies, waits for them, and re-layouts  1.41 us
    squeeze x1, local copies, waits for them, and re-layouts, on_device(): regrid_weights[0]  1.35 us
    squeeze x1, local copies, waits for them, and re-layouts, on_device(): regrid_rows[0]  1.35 us

profile of v3, /device:TPU:0, one launch (start us, length us, event | category | flops | bytes accessed | tf_op | source)
XLA Modules:
  0.0 62.9 jit_solution(16483060289143621780)
XLA Ops:
  0.0 0.7 %pad_maximum_fusion = f32[160,3]{0,1:T(4,128)S(1)} fusion(f32[160,1]{0,1:T(1,128)} %bitcast.24, f32[160,1]{0,1:T(1,128)} %bitcast.25, f32[160,1]{0,1:T(1,128)} %bitcast.26), kind=kLoop, calls=%fused_computation | loop fusion | flops 960 | bytes 3840 | tf_op jit(solution)/shard_map/stack | solution.py:341
  0.7 1.4 %copy.23.rows_ref = s32[16,4]{1,0:T(8,128)} copy(s32[16,4]{0,1:T(4,128)} %bitcast.22) | data formatting | bytes 512 | tf_op jit(solution)/shard_map/squeeze | solution.py:395
  2.1 1.4 %copy.24.weights_ref = f32[16,4]{1,0:T(8,128)} copy(f32[16,4]{0,1:T(4,128)} %bitcast.23) | data formatting | bytes 512 | tf_op jit(solution)/shard_map/squeeze | solution.py:395
  3.4 1.4 %copy.22 = bf16[1,8,160]{1,2,0:T(8,128)(2,1)} copy(bf16[1,8,160]{2,1,0:T(8,128)(2,1)} %param.18) | data formatting | bytes 5120 | tf_op args[7]
  4.8 0.8 %copy.21.vec_ref = f32[160,3]{1,0:T(8,128)} copy(f32[160,3]{0,1:T(4,128)S(1)} %pad_maximum_fusion) | data formatting | bytes 3840 | tf_op jit(solution)/shard_map/stack | solution.py:341
  5.6 51.4 %convolutions.1 = (bf16[2560,768]{1,0:T(8,128)(2,1)}, bf16[16,8,768]{2,1,0:T(8,128)(2,1)}, bf16[16,8,768]{2,1,0:T(8,128)(2,1)}, bf16[16,8,768]{2,1,0:T(8,128)(2,1)}) custom-call(bf16[160,16,768]{2,1,0:T(8,128)(2,1)} %bitcast.16, bf16[3,3,160,160]{3,2,1,0:T(8,128)(2,1)} %bitcast.17, bf16[3,3,160,160]{3,2,1,0:T(8,128)(2,1)} %bitcast.18, ...), custom_call_target="tpu_custom_call" | custom-call | tf_op jit(solution)/shard_map/convolutions/pallas_call | solution.py:346
  57.0 5.9 %exchange.1 = bf16[160,16,768]{2,1,0:T(8,128)(2,1)} custom-call(s32[16,4]{1,0:T(8,128)} %copy.23.rows_ref, f32[16,4]{1,0:T(8,128)} %copy.24.weights_ref, bf16[2560,768]{1,0:T(8,128)(2,1)} %get-tuple-element.9.hid_ref, bf16[16,8,768]{2,1,0:T(8,128)(2,1)} %get-tuple-element.10.up_ref, bf16[16,8,768]{2,1,0:T(8,128)(2,1)} %get-tuple-element.11.mid_ref, ...), custom_call_target="tpu_custom_call" | custom-call | tf_op jit(solution)/shard_map/exchange/pallas_call | solution.py:374
